TPU v7x, 32 devices: a whole 2x2x4 slice. The times are simulated.
32 devices in a mesh: dp: 4 (over y, x), expert: 8 (over z, core).
Axes of the slice: x: 2, y: 2, z: 4, core: 2. Of those that a mesh axis runs over, the one named last changes fastest.
Arguments:
- tokens: bfloat16 [8192, 2048], P(('dp', 'expert')), may hold values from -6 to 6
- out_grad: bfloat16 [8192, 2048], P(('dp', 'expert')), may hold values from -6 to 6
- token_picks: int32 [32, 16, 8], P(('dp', 'expert')), may hold values from 0 to 255, as said below
- router: bfloat16 [2048, 16], P(None, 'expert'), may hold values from -0.125 to 0.125
- kept_blocks: int32 [16, 3, 128], P('expert'), may hold values from 0 to 384, as said below
- masters: float32 [16, 3, 128, 4096], P('expert', None, 'dp'), may hold values from -0.25 to 0.25
- scores: float32 [16, 3, 128], P('expert', None, 'dp'), may hold values from -6 to 6
Outputs:
- layer_out: bfloat16 [8192, 2048], P(('dp', 'expert'))
- input_grad: bfloat16 [8192, 2048], P(('dp', 'expert'))
- master_new: float32 [16, 3, 128, 4096], P('expert', None, 'dp')
- score_new: float32 [16, 3, 128], P('expert', None, 'dp')
- router_grad: float32 [2048, 16], P('dp', 'expert')
Inputs may be any that keep to these rules, and one draw needn't show every extreme that they name: `token_picks`: within one source block and one expert the 8 picks are distinct tokens. `kept_blocks`: each list of 128 slots holds, in ascending order, between 64 and 128 distinct block numbers below 384, then 384 in the remaining slots; for each of the three matrices the list of some expert is full.
All inputs are finite; a program needn't handle non-finite values.
Results may differ from a plain program's by a relative error of at most 0.0081.
Values may be sent and summed in bfloat16 or wider, within the bound.
A program may use at most 192 MiB of HBM per device.

v0:
```python
import jax
import jax.numpy as jnp
from jax import lax
from jax.sharding import PartitionSpec as P

FF = 768
BS = 64


LEARN_RATE = 0.005
SCORE_RATE = 0.05


def layouts(kept_rows, in_blocks, hid_blocks):
    blocks_total = in_blocks * hid_blocks
    plan_list = []
    for matrix, col_count in ((0, hid_blocks), (1, hid_blocks), (2, in_blocks)):
        usable = kept_rows[matrix] < blocks_total
        safe_index = jnp.where(usable, kept_rows[matrix], 0)
        plan_list.append((safe_index // col_count, safe_index % col_count, usable, safe_index))
    return plan_list


def masked_tiles(tile_stack, plan_list):
    return [
        jnp.where(
            plan_list[matrix][2][:, None, None],
            tile_stack[matrix],
            jnp.zeros_like(tile_stack[matrix]),
        )
        for matrix in range(3)
    ]


def block_matrix(tile_set, block_plan, row_blocks, col_blocks):
    tile_width = tile_set.shape[-1]
    slot_count = tile_set.shape[0]
    numbers = jnp.arange(row_blocks * col_blocks, dtype=jnp.int32)
    hits = (block_plan[3][None, :] == numbers[:, None]) & block_plan[2][None, :]
    slot_of = jnp.sum(jnp.where(hits, jnp.arange(slot_count, dtype=jnp.int32)[None, :], 0), axis=1)
    present = jnp.any(hits, axis=1)
    slot_of = jnp.where(present, slot_of, slot_count)
    padded = jnp.concatenate(
        [tile_set, jnp.zeros((1, tile_width, tile_width), tile_set.dtype)], axis=0
    )
    placed = jnp.take(padded, slot_of, axis=0).reshape(
        row_blocks, col_blocks, tile_width, tile_width
    )
    return placed.transpose(0, 2, 1, 3).reshape(row_blocks * tile_width, col_blocks * tile_width)


def project(operand, weight, flipped):
    tile_set, block_plan, matrix_full = weight
    if flipped:
        return lax.dot_general(
            operand, matrix_full, (((1,), (1,)), ((), ())), preferred_element_type=jnp.float32
        )
    return jnp.dot(operand, matrix_full, preferred_element_type=jnp.float32)


def weight_grad(operand, cotangent, weight):
    tile_set, block_plan, matrix_full = weight
    tile_width = tile_set.shape[-1]
    grid_rows = matrix_full.shape[0] // tile_width
    grid_cols = matrix_full.shape[1] // tile_width
    full_grad = lax.dot_general(
        operand, cotangent, (((0,), (0,)), ((), ())), preferred_element_type=jnp.float32
    )
    full_grad = full_grad.reshape(grid_rows, tile_width, grid_cols, tile_width).transpose(
        0, 2, 1, 3
    )
    gradient = jnp.take(full_grad.reshape(-1, tile_width, tile_width), block_plan[3], axis=0)
    gradient = jnp.where(block_plan[2][:, None, None], gradient, jnp.zeros_like(gradient))
    return gradient.reshape(-1, tile_width * tile_width)


def expert_forward(rows_in, weights, router_col):
    gate_pre = project(rows_in, weights[0], False)
    up_pre = project(rows_in, weights[1], False)
    hidden = (jax.nn.silu(gate_pre) * up_pre).astype(jnp.bfloat16)
    output = project(hidden, weights[2], False)
    gating = jax.nn.sigmoid(jnp.dot(rows_in, router_col, preferred_element_type=jnp.float32))
    part_out = (gating[:, None] * output).astype(jnp.bfloat16)
    return (part_out, (gate_pre, up_pre, hidden, output, gating))


def expert_down_grad(grad_rows, saved_state, weights):
    gate_pre, up_pre, hidden, output, gating = saved_state
    grad_float = grad_rows.astype(jnp.float32)
    logit_grad = jnp.sum(grad_float * output, axis=1) * gating * (1.0 - gating)
    scaled = (gating[:, None] * grad_float).astype(jnp.bfloat16)
    down_grad = weight_grad(hidden, scaled, weights[2])
    hidden_grad = project(scaled, weights[2], True)
    return (down_grad, (hidden_grad, logit_grad))


def expert_rest_grad(rows_in, carried, saved_state, weights, router_col):
    hidden_grad, logit_grad = carried
    gate_pre, up_pre = (saved_state[0], saved_state[1])
    sigmoid = jax.nn.sigmoid(gate_pre)
    gate_grad = (hidden_grad * up_pre * sigmoid * (1.0 + gate_pre * (1.0 - sigmoid))).astype(
        jnp.bfloat16
    )
    up_grad = (hidden_grad * gate_pre * sigmoid).astype(jnp.bfloat16)
    gate_weight = weight_grad(rows_in, gate_grad, weights[0])
    up_weight = weight_grad(rows_in, up_grad, weights[1])
    input_part = project(gate_grad, weights[0], True) + project(up_grad, weights[1], True)
    input_part = input_part + logit_grad[:, None] * router_col.astype(jnp.float32)[None, :]
    router_part = jnp.dot(logit_grad, rows_in.astype(jnp.float32), precision=lax.Precision.HIGHEST)
    return (input_part.astype(jnp.bfloat16), gate_weight, up_weight, router_part)


def body(tokens, out_grad, token_picks, router, kept_blocks, masters, scores):
    local_count = kept_blocks.shape[0]
    peer_count = lax.axis_size("expert")
    capacity = token_picks.shape[2]
    model_width = tokens.shape[1]
    in_blocks = model_width // BS
    hid_blocks = FF // BS
    copies = lax.all_gather(masters.astype(jnp.bfloat16), "dp", axis=2, tiled=True)
    copies = copies.reshape(local_count, 3, -1, BS, BS)
    slot_order = (
        token_picks[0].reshape(peer_count, local_count, capacity).transpose(1, 0, 2).reshape(-1)
    )
    experts = []
    for member in range(local_count):
        plan_list = layouts(kept_blocks[member], in_blocks, hid_blocks)
        tile_list = masked_tiles(copies[member], plan_list)
        extents = ((in_blocks, hid_blocks), (in_blocks, hid_blocks), (hid_blocks, in_blocks))
        matrix_list = [
            block_matrix(
                tile_list[matrix], plan_list[matrix], extents[matrix][0], extents[matrix][1]
            )
            for matrix in range(3)
        ]
        experts.append(
            [(tile_list[matrix], plan_list[matrix], matrix_list[matrix]) for matrix in range(3)]
        )

    def outbound(source):
        return jnp.take(source, slot_order, axis=0).reshape(
            local_count, peer_count, capacity, model_width
        )

    arrived = lax.all_to_all(outbound(tokens), "expert", split_axis=1, concat_axis=1, tiled=True)
    parts_out = []
    saved_list = []
    for member in range(local_count):
        rows_in = arrived[member].reshape(-1, model_width)
        part_out, saved_state = expert_forward(rows_in, experts[member], router[:, member])
        parts_out.append(part_out.reshape(peer_count, capacity, model_width))
        saved_list.append(saved_state)
    parts_out, saved_list = (jnp.stack(parts_out), saved_list)
    returned_out, arrived_grad = (
        lax.all_to_all(parts_out, "expert", split_axis=1, concat_axis=1, tiled=True),
        lax.all_to_all(outbound(out_grad), "expert", split_axis=1, concat_axis=1, tiled=True),
    )
    down_list = []
    inner_list = []
    for member in range(local_count):
        grad_rows = arrived_grad[member].reshape(-1, model_width)
        down_grad, inner_state = expert_down_grad(grad_rows, saved_list[member], experts[member])
        down_list.append(down_grad)
        inner_list.append(inner_state)
    parts_in = []
    gate_list = []
    up_list = []
    router_list = []
    for member in range(local_count):
        rows_in = arrived[member].reshape(-1, model_width)
        input_part, gate_weight, up_weight, router_part = expert_rest_grad(
            rows_in, inner_list[member], saved_list[member], experts[member], router[:, member]
        )
        parts_in.append(input_part.reshape(peer_count, capacity, model_width))
        gate_list.append(gate_weight)
        up_list.append(up_weight)
        router_list.append(router_part)
    router_terms = jnp.stack(router_list, axis=1)
    all_terms = jnp.stack([jnp.stack(gate_list), jnp.stack(up_list), jnp.stack(down_list)], axis=1)
    summed = lax.psum_scatter(all_terms, "dp", scatter_dimension=2, tiled=True)
    router_sum = lax.psum_scatter(router_terms, "dp", scatter_dimension=0, tiled=True)
    parts_in, summed, router_sum = (jnp.stack(parts_in), summed, router_sum)
    returned_in = lax.all_to_all(parts_in, "expert", split_axis=1, concat_axis=1, tiled=True)

    def combine(returned):
        totals = jnp.zeros((tokens.shape[0], model_width), jnp.float32)
        totals = totals.at[slot_order].add(returned.reshape(-1, model_width).astype(jnp.float32))
        return totals.astype(jnp.bfloat16)

    master_new = masters - LEARN_RATE * summed
    score_new = scores - SCORE_RATE * jnp.sum(masters * summed, axis=-1)
    return (combine(returned_out), combine(returned_in), master_new, score_new, router_sum)


def solution(mesh):
    return jax.shard_map(
        body,
        mesh=mesh,
        in_specs=(
            P(("dp", "expert"), None),
            P(("dp", "expert"), None),
            P(("dp", "expert"), None, None),
            P(None, "expert"),
            P("expert", None, None),
            P("expert", None, "dp", None),
            P("expert", None, "dp"),
        ),
        out_specs=(
            P(("dp", "expert"), None),
            P(("dp", "expert"), None),
            P("expert", None, "dp", None),
            P("expert", None, "dp"),
            P("dp", "expert"),
        ),
        check_vma=False,
    )
```

profile of v0, /device:TPU:0, one launch (start us, length us, event | category | flops | bytes accessed | tf_op | source)
XLA Modules:
  0.0 854.5 jit_solution(10335299297657056716)
XLA Ops:
  7.2 5.5 copy.318
  16.4 6.3 all-to-all-start
  45.1 40.7 %all-gather.2.cloned.1.call-done = bf16[2,3,128,4096]{3,0,1,2:T(2,128)(2,1)} async-done(((bf16[2,3,32,4096]{3,0,1,2:T(2,128)(2,1)}), bf16[2,3,128,4096]{3,0,1,2:T(2,128)(2,1)}) %all-gather.2.cloned.1.call-update) | async-done | bytes 6291472 | tf_op jit(solution)/shard_map/all_gather | solution.py:120
  85.8 18.9 %fusion.119 = (bf16[1,1,128,4096]{3,0,1,2:T(2,128)(2,1)}, bf16[1,1,128,4096]{3,0,1,2:T(2,128)(2,1)}, bf16[1,1,128,4096]{3,0,1,2:T(2,128)(2,1)}, bf16[1,1,128,409...) fusion(bf16[2,3,128,4096]{3,0,1,2:T(2,128)(2,1)} %all-gather.2.cloned.1.call-done), kind=kLoop, calls=%fused_computation.264 | loop fusion | bytes 12582912 | tf_op jit(solution)/shard_map/slice | solution.py:28
  104.7 5.4 copy.310
  140.6 5.6 gather_fusion.3
  146.3 7.0 broadcast_select_fusion.3
  153.3 13.5 %gather_fusion.2 = bf16[384,64,64]{2,1,0:T(8,128)(2,1)} fusion(bf16[129,64,64]{2,1,0:T(8,128)(2,1)S(1)} %concatenate.19, s32[1024]{0:T(1024)S(1)} %pad_clamp_fusion.10), kind=kCustom, calls=%fused_computation.4.clone | custom fusion | bytes 6292992 | tf_op jit(solution)/shard_map/jit(_take)/gather | solution.py:46
  166.9 8.0 broadcast_select_fusion.4
  176.4 7.7 copy.253
  184.1 9.7 %reshape.313 = bf16[768,2048]{1,0:T(8,128)(2,1)} reshape(bf16[12,64,32,64]{3,2,1,0:T(8,128)(2,1)} %copy.253) | data formatting | bytes 6291456 | tf_op jit(solution)/shard_map/reshape | solution.py:49
  193.8 9.4 %copy.250 = bf16[32,64,12,64]{1,0,3,2:T(8,128)(2,1)} copy(bf16[32,64,12,64]{3,1,2,0:T(8,128)(2,1)} %bitcast.386) | data formatting | bytes 6291456 | tf_op jit(solution)/shard_map/transpose | solution.py:49
  203.2 9.9 %reshape.311 = bf16[2048,768]{0,1:T(8,128)(2,1)} reshape(bf16[32,64,12,64]{1,0,3,2:T(8,128)(2,1)} %copy.250) | data formatting | bytes 6291456 | tf_op jit(solution)/shard_map/reshape | solution.py:49
  215.3 13.0 %gather_fusion.1 = bf16[384,64,64]{2,1,0:T(8,128)(2,1)} fusion(bf16[129,64,64]{2,1,0:T(8,128)(2,1)S(1)} %concatenate.18, s32[1024]{0:T(1024)S(1)} %pad_clamp_fusion.11), kind=kCustom, calls=%fused_computation.1.clone | custom fusion | bytes 6292992 | tf_op jit(solution)/shard_map/jit(_take)/gather | solution.py:46
  228.3 7.0 broadcast_select_fusion.5
  235.4 9.4 %copy.247 = bf16[32,64,12,64]{1,0,3,2:T(8,128)(2,1)} copy(bf16[32,64,12,64]{3,1,2,0:T(8,128)(2,1)} %bitcast.387) | data formatting | bytes 6291456 | tf_op jit(solution)/shard_map/transpose | solution.py:49
  244.8 9.7 %reshape.309 = bf16[2048,768]{0,1:T(8,128)(2,1)} reshape(bf16[32,64,12,64]{1,0,3,2:T(8,128)(2,1)} %copy.247) | data formatting | bytes 6291456 | tf_op jit(solution)/shard_map/reshape | solution.py:49
  274.6 13.1 %gather_fusion.6 = bf16[384,64,64]{2,1,0:T(8,128)(2,1)} fusion(bf16[129,64,64]{2,1,0:T(8,128)(2,1)S(1)} %concatenate.23, s32[1024]{0:T(1024)} %pad_clamp_fusion.6), kind=kCustom, calls=%fused_computation.8.clone | custom fusion | bytes 6292992 | tf_op jit(solution)/shard_map/jit(_take)/gather | solution.py:46
  292.2 7.7 copy.263
  299.9 9.9 %reshape.319 = bf16[768,2048]{1,0:T(8,128)(2,1)} reshape(bf16[12,64,32,64]{3,2,1,0:T(8,128)(2,1)} %copy.263) | data formatting | bytes 6291456 | tf_op jit(solution)/shard_map/reshape | solution.py:49
  318.1 13.2 %gather_fusion.5 = bf16[384,64,64]{2,1,0:T(8,128)(2,1)} fusion(bf16[129,64,64]{2,1,0:T(8,128)(2,1)S(1)} %concatenate.22, s32[1024]{0:T(1024)} %pad_clamp_fusion.7), kind=kCustom, calls=%fused_computation.7.clone | custom fusion | bytes 6292992 | tf_op jit(solution)/shard_map/jit(_take)/gather | solution.py:46
  331.3 7.0 broadcast_select_fusion.1
  338.3 9.4 %copy.260 = bf16[32,64,12,64]{1,0,3,2:T(8,128)(2,1)} copy(bf16[32,64,12,64]{3,1,2,0:T(8,128)(2,1)} %bitcast.389) | data formatting | bytes 6291456 | tf_op jit(solution)/shard_map/transpose | solution.py:49
  347.7 9.9 %reshape.317 = bf16[2048,768]{0,1:T(8,128)(2,1)} reshape(bf16[32,64,12,64]{1,0,3,2:T(8,128)(2,1)} %copy.260) | data formatting | bytes 6291456 | tf_op jit(solution)/shard_map/reshape | solution.py:49
  365.9 13.3 %gather_fusion.4 = bf16[384,64,64]{2,1,0:T(8,128)(2,1)} fusion(bf16[129,64,64]{2,1,0:T(8,128)(2,1)S(1)} %concatenate.21, s32[1024]{0:T(1024)} %pad_clamp_fusion.8), kind=kCustom, calls=%fused_computation.6.clone | custom fusion | bytes 6292992 | tf_op jit(solution)/shard_map/jit(_take)/gather | solution.py:46
  379.1 7.0 broadcast_select_fusion.2
  386.1 9.4 %copy.257 = bf16[32,64,12,64]{1,0,3,2:T(8,128)(2,1)} copy(bf16[32,64,12,64]{3,1,2,0:T(8,128)(2,1)} %bitcast.390) | data formatting | bytes 6291456 | tf_op jit(solution)/shard_map/transpose | solution.py:49
  395.5 10.1 %reshape.315 = bf16[2048,768]{0,1:T(8,128)(2,1)} reshape(bf16[32,64,12,64]{1,0,3,2:T(8,128)(2,1)} %copy.257) | data formatting | bytes 6291456 | tf_op jit(solution)/shard_map/reshape | solution.py:49
  419.5 7.3 fusion.125
  426.8 7.4 gather_fusion.13
  434.3 6.3 fusion.124
  440.6 7.5 gather_fusion.12
  448.1 6.1 select_select_fusion
  466.3 7.4 fusion.123
  473.7 7.4 gather_fusion.11
  481.2 7.3 fusion.122
  488.4 7.5 gather_fusion.10
  495.9 6.1 select_select_fusion.2
  513.3 7.4 fusion.121
  522.5 7.3 fusion.120
  529.7 7.5 gather_fusion.9
  537.3 7.5 gather_fusion.8
  544.8 6.1 select_select_fusion.4
  573.2 19.4 %copy.287 = f32[2,3,128,4096]{3,0,1,2:T(2,128)} copy(f32[2,3,128,4096]{2,3,0,1:T(8,128)} %pad_maximum_fusion) | data formatting | bytes 25165824 | tf_op jit(solution)/shard_map/stack | solution.py:179
  607.9 6.7 all-to-all-done.1
  625.2 8.2 all-to-all-done.3
  637.3 197.1 %all-reduce.9.cloned.1.call-done = f32[2,3,128,4096]{3,0,1,2:T(2,128)} async-done(((f32[2,3,128,4096]{3,0,1,2:T(2,128)}), f32[2,3,128,4096]{3,0,1,2:T(2,128)}) %all-reduce.9.cloned.1.call-update) | async-done | bytes 12582928
  834.4 9.1 %multiply_reduce_fusion = (f32[2,3,32]{0,1,2:T(4,128)S(1)}, f32[2,3,32,4096]{3,0,1,2:T(2,128)S(1)}) fusion(f32[2,3,128,4096]{3,0,1,2:T(2,128)} %all-reduce.9.cloned.1.call-done, u32[]{:T(128)S(6)} %multiply.1, f32[2,3,32,4096]{3,2,1,0:T(8,128)} %param.18), kind=kLoop, calls=%fused_computation.32 | loop fusion | flops 3145536 | bytes 9437956 | tf_op jit(solution)/shard_map/reduce_sum | solution.py:191
  (282 shorter events, 195.5 us)
Async XLA Ops:
  7.2 78.6 %all-gather.2.cloned.1.call-start = ((), (), s32[]{:S(2)}) async-start(), calls=%async_computation.5 | async-start | bytes 7864320 | tf_op jit(solution)/shard_map/all_gather | solution.py:120
  14.4 8.3 copy-start.58
  15.4 27.2 %copy-start.30 = (bf16[2048,2]{0,1:T(2,128)(2,1)S(1)}, bf16[2048,2]{0,1:T(2,128)(2,1)}, u32[]{:S(2)}) copy-start(bf16[2048,2]{0,1:T(2,128)(2,1)} %param.16) | copy-start | bytes 24580
  16.4 21.7 %all-to-all-start = ((bf16[2,8,8,2048]{3,2,0,1:T(8,128)(2,1)}), bf16[2,8,8,2048]{3,2,0,1:T(8,128)(2,1)S(1)}, u32[]{:S(2)}, u32[]{:S(2)}) async-start(bf16[2,8,8,2048]{3,2,0,1:T(8,128)(2,1)} %copy.242), calls=%async_computation | async-start | bytes 1048576 | tf_op jit(solution)/shard_map/all_to_all | solution.py:145
  23.4 19.7 %copy-start.33 = (pred[128]{0:T(512)(128)(4,1)}, pred[128]{0:T(512)(128)(4,1)S(1)}, u32[]{:S(2)}) copy-start(pred[128]{0:T(512)(128)(4,1)S(1)} %get-tuple-element.96) | copy-start | bytes 388
  23.4 81.3 %copy-start.40 = (pred[128]{0:T(512)(128)(4,1)}, pred[128]{0:T(512)(128)(4,1)S(1)}, u32[]{:S(2)}) copy-start(pred[128]{0:T(512)(128)(4,1)S(1)} %get-tuple-element.101) | copy-start | bytes 388
  23.4 81.3 %copy-start.45 = (pred[128]{0:T(512)(128)(4,1)}, pred[128]{0:T(512)(128)(4,1)S(1)}, u32[]{:S(2)}) copy-start(pred[128]{0:T(512)(128)(4,1)S(1)} %get-tuple-element.100) | copy-start | bytes 388
  23.4 91.4 %copy-start.43 = (pred[128]{0:T(512)(128)(4,1)}, pred[128]{0:T(512)(128)(4,1)S(1)}, u32[]{:S(2)}) copy-start(pred[128]{0:T(512)(128)(4,1)S(1)} %get-tuple-element.97) | copy-start | bytes 388
  23.4 102.9 %copy-start.38 = (pred[128]{0:T(512)(128)(4,1)}, pred[128]{0:T(512)(128)(4,1)S(1)}, u32[]{:S(2)}) copy-start(pred[128]{0:T(512)(128)(4,1)S(1)} %get-tuple-element.98) | copy-start | bytes 388
  23.4 151.5 %copy-start.36 = (pred[128]{0:T(512)(128)(4,1)}, pred[128]{0:T(512)(128)(4,1)S(1)}, u32[]{:S(2)}) copy-start(pred[128]{0:T(512)(128)(4,1)S(1)} %get-tuple-element.99) | copy-start | bytes 388
  38.1 219.4 %all-to-all-start.2 = ((bf16[2,8,8,2048]{3,2,0,1:T(8,128)(2,1)}), bf16[2,8,8,2048]{3,2,0,1:T(8,128)(2,1)}, u32[]{:S(2)}, u32[]{:S(2)}) async-start(bf16[2,8,8,2048]{3,2,0,1:T(8,128)(2,1)} %copy.267), calls=%async_computation.2 | async-start | bytes 1048576 | tf_op jit(solution)/shard_map/all_to_all | solution.py:156
  42.3 577.4 %reduce-scatter.4.cloned.1.call-start = ((), (), s32[]{:S(2)}) async-start(), calls=%async_computation.6 | async-start | bytes 1310720
  42.8 61.9 %copy-start.52 = (f32[64]{0:T(128)}, f32[64]{0:T(128)S(1)}, u32[]{:S(2)}) copy-start(f32[64]{0:T(128)S(1)} %fusion.13) | copy-start | bytes 772
  43.1 61.6 %copy-start.54 = (f32[64]{0:T(128)}, f32[64]{0:T(128)S(1)}, u32[]{:S(2)}) copy-start(f32[64]{0:T(128)S(1)} %fusion.9) | copy-start | bytes 772
  166.8 9.6 %slice-start = ((s8[6291456]{0:T(1024)(128)(4,1)}), s8[4194304]{0:T(1024)(128)(4,1)S(1)}, s32[]{:S(2)}) async-start(s8[6291456]{0:T(1024)(128)(4,1)} %bitcast.383), calls=%async_computation.8 | async-start | bytes 8388608
  166.8 8.0 copy-start.14
  166.9 9.6 %slice-start.1 = ((s8[6291456]{0:T(1024)(128)(4,1)}), s8[2097152]{0:T(1024)(128)(4,1)S(1)}, s32[]{:S(2)}) async-start(s8[6291456]{0:T(1024)(128)(4,1)} %bitcast.383), calls=%async_computation.9 | async-start | bytes 4194304
  257.5 7.2 copy-start.5
  264.6 9.2 %copy-start.46 = (pred[128]{0:T(512)(128)(4,1)S(1)}, pred[128]{0:T(512)(128)(4,1)}, u32[]{:S(2)}) copy-start(pred[128]{0:T(512)(128)(4,1)} %copy-done.45) | copy-start | bytes 388
  299.9 9.9 %copy-start.8 = (bf16[1,1,128,4096]{3,0,1,2:T(2,128)(2,1)S(1)}, bf16[1,1,128,4096]{3,0,1,2:T(2,128)(2,1)}, u32[]{:S(2)}) copy-start(bf16[1,1,128,4096]{3,0,1,2:T(2,128)(2,1)} %get-tuple-element.69) | copy-start | bytes 3145732
  309.8 7.5 copy-start.41
  347.7 9.9 %copy-start.7 = (bf16[1,1,128,4096]{3,0,1,2:T(2,128)(2,1)S(1)}, bf16[1,1,128,4096]{3,0,1,2:T(2,128)(2,1)}, u32[]{:S(2)}) copy-start(bf16[1,1,128,4096]{3,0,1,2:T(2,128)(2,1)} %get-tuple-element.70) | copy-start | bytes 3145732
  357.5 7.5 copy-start.34
  395.5 13.2 %copy-start.32 = (f32[8,8]{1,0:T(8,128)S(1)}, f32[8,8]{1,0:T(8,128)}, u32[]{:S(2)}) copy-start(f32[8,8]{1,0:T(8,128)} %mul.221) | copy-start | bytes 772
  408.7 10.1 %copy-start.16 = (f32[64,768]{1,0:T(8,128)}, f32[64,768]{1,0:T(8,128)S(1)}, u32[]{:S(2)}) copy-start(f32[64,768]{1,0:T(8,128)S(1)} %fusion.41) | copy-start | bytes 589828
  411.9 6.9 copy-start.22
  413.8 13.0 %copy-start.18 = (f32[64,768]{1,0:T(8,128)}, f32[64,768]{1,0:T(8,128)S(1)}, u32[]{:S(2)}) copy-start(f32[64,768]{1,0:T(8,128)S(1)} %get-tuple-element.104) | copy-start | bytes 589828
  440.6 7.5 copy-start.44
  440.6 7.5 copy-start.47
  440.6 7.5 copy-start.61
  440.6 7.5 copy-start.62
  488.4 7.5 copy-start.39
  488.4 7.5 copy-start.42
  537.3 7.5 copy-start.35
  537.3 7.5 copy-start.37
  537.3 7.5 copy-start.59
  537.3 7.5 copy-start.60
  562.9 271.5 %all-reduce.9.cloned.1.call-start = ((), (), s32[]{:S(2)}) async-start(), calls=%async_computation.7 | async-start | bytes 25165824
  592.6 6.7 copy-start.17
  592.6 6.7 copy-start.19
  592.6 6.7 copy-start.23
  593.3 9.6 %copy-start.51 = (f32[64]{0:T(128)S(1)}, f32[64]{0:T(128)}, u32[]{:S(2)}) copy-start(f32[64]{0:T(128)} %copy-done.50) | copy-start | bytes 772
  594.5 20.2 %all-to-all-start.1 = ((bf16[2,8,8,2048]{3,2,0,1:T(8,128)(2,1)}), bf16[2,8,8,2048]{3,2,0,1:T(8,128)(2,1)S(1)}, u32[]{:S(2)}, u32[]{:S(2)}) async-start(bf16[2,8,8,2048]{3,2,0,1:T(8,128)(2,1)} %pad_maximum_fusion.1), calls=%async_computation.1 | async-start | bytes 1048576 | tf_op jit(solution)/shard_map/all_to_all | solution.py:155
  606.4 11.8 %copy-start.29 = (s32[2,8,8]{2,1,0:T(8,128)S(1)}, s32[2,8,8]{2,1,0:T(8,128)}, u32[]{:S(2)}) copy-start(s32[2,8,8]{2,1,0:T(8,128)} %copy-done.28) | copy-start | bytes 1540
  606.4 11.9 %copy-start.65 = (u32[32]{0:T(128)S(1)}, u32[32]{0:T(128)}, u32[]{:S(2)}) copy-start(u32[32]{0:T(128)} %constant.77) | copy-start | bytes 388
  606.4 13.1 %copy-start.57 = (f32[2,3,32]{2,0,1:T(2,128)S(1)}, f32[2,3,32]{2,0,1:T(2,128)}, u32[]{:S(2)}) copy-start(f32[2,3,32]{2,0,1:T(2,128)} %param.19) | copy-start | bytes 2308
  614.6 18.8 %all-to-all-start.3 = ((bf16[2,8,8,2048]{3,2,0,1:T(8,128)(2,1)}), bf16[2,8,8,2048]{3,2,0,1:T(8,128)(2,1)S(1)}, u32[]{:S(2)}, u32[]{:S(2)}) async-start(bf16[2,8,8,2048]{3,2,0,1:T(8,128)(2,1)} %pad_maximum_fusion.2), calls=%async_computation.3 | async-start | bytes 1048576 | tf_op jit(solution)/shard_map/all_to_all | solution.py:183
  834.4 13.3 %copy-start.1 = (bf16[256,2048]{1,0:T(8,128)(2,1)S(1)}, bf16[256,2048]{1,0:T(8,128)(2,1)}, u32[]{:S(2)}) copy-start(bf16[256,2048]{1,0:T(8,128)(2,1)} %param.14) | copy-start | bytes 3145732
  (27 other events, 102.8 us)
Sparse Core Ops, SparseCore 0:
  12.9 72.8 all-gather.1
  563.0 27.8 reduce-scatter.3
  594.8 239.5 all-reduce.8
where the time goes:
time: 863 us; the launch traced here: 854 us
  local copies, waits for them, and re-layouts  385 us (45%)
  waiting for transfers between devices  258 us (30%)
  other arithmetic  102 us (12%)
  matrix products  75.2 us (9%)
  starting transfers between devices  19.2 us (2%)
  between operations  15.6 us (2%)
    unnamed x5, waiting for transfers between devices  197 us
    gather x6, local copies, waits for them, and re-layouts, block_matrix(): jnp.take(padded, slot_of, axis=0)  71.8 us
    reshape x6, local copies, waits for them, and re-layouts, block_matrix(): placed.transpose(0, 2, 1, 3)  59.2 us
    transpose x6, local copies, waits for them, and re-layouts, block_matrix(): placed.transpose(0, 2, 1, 3)  52.9 us
    gather x6, local copies, waits for them, and re-layouts, weight_grad(): jnp.take(full_grad.reshape(-1, tile_width, tile_width), block_plan[3], ax...  44.9 us
    unnamed x150, local copies, waits for them, and re-layouts  43.3 us
    dot_general x6, matrix products, weight_grad(): lax.dot_general(operand, cotangent, (((0,), (0,)), ((), ())), preferred_e...  43 us
    all_gather x1, waiting for transfers between devices, body(): lax.all_gather(masters.astype(jnp.bfloat16), 'dp', axis=2, tiled=True)  40.7 us
  transfers between devices with their start and end apart: 7, of which 5 were waited for; matrix products, arithmetic and copies ran while one was open for 27% of the time, Pallas kernels for 0%

commit v1 on v0

v1 whole, which is shorter than its diff:
```python
import functools

import jax
import jax.numpy as jnp
from jax import lax
from jax.experimental import pallas as pl
from jax.experimental.pallas import tpu as pltpu
from jax.sharding import PartitionSpec as P

FF = 768
BS = 64
LANES = 2 * BS

LEARN_RATE = 0.005
SCORE_RATE = 0.05

F32 = jnp.float32
BF16 = jnp.bfloat16


def dot(a, b, dims=((1,), (0,))):
    return lax.dot_general(a, b, (dims, ((), ())), preferred_element_type=F32)


def sigma(v):
    return 1.0 / (1.0 + jnp.exp(-v))


def kernel(
    sizes,
    place_ref,
    pick_ref,
    picks_col,
    picks_row,
    tokens,
    out_grad,
    router,
    own,
    layer_out,
    input_grad,
    grads,
    router_out,
    held,
    stage,
    w_gate,
    w_up,
    w_down,
    dense,
    got,
    x_send,
    x_got,
    y_send,
    y_got,
    rows,
    scaled,
    hidden,
    pre_gate,
    pre_up,
    outs,
    r_send,
    r_got,
    w_ssem,
    w_rsem,
    g_ssem,
    g_rsem,
    x_ssem,
    x_rsem,
    y_ssem,
    y_rsem,
    r_ssem,
    r_rsem,
):
    n_dp, n_ex, members, cap = sizes
    width = tokens.shape[1]
    in_blocks = width // BS
    hid_blocks = FF // BS
    blocks = in_blocks * hid_blocks
    pairs = own.shape[1]
    total_pairs = pairs * n_dp
    slots = 2 * total_pairs
    per_peer = members * cap
    all_rows = n_ex * per_peer
    expert_rows = n_ex * cap
    my_dp = lax.axis_index("dp")
    my_ex = lax.axis_index("expert")

    def ahead(i):
        return lax.rem(my_dp + i, n_dp)

    def behind(i):
        return lax.rem(my_dp + n_dp - i, n_dp)

    def peer(i):
        return lax.rem(my_ex + i, n_ex)

    def source(i):
        return lax.rem(my_ex + n_ex - i, n_ex)

    def loop(lo, hi, fn):
        def step(i, carry):
            fn(i)
            return carry

        lax.fori_loop(lo, hi, step, 0)

    barrier = pltpu.get_barrier_semaphore()
    for i in range(1, n_dp):
        pl.semaphore_signal(
            barrier, inc=1, device_id={"dp": ahead(i)}, device_id_type=pl.DeviceIdType.MESH
        )
    loop(
        1,
        n_ex,
        lambda i: pl.semaphore_signal(
            barrier, inc=1, device_id={"expert": peer(i)}, device_id_type=pl.DeviceIdType.MESH
        ),
    )

    chosen = (
        lax.broadcasted_iota(jnp.int32, (all_rows, tokens.shape[0]), 1) == picks_col[...]
    ).astype(F32).astype(BF16)
    x_send[0] = dot(chosen, tokens[...]).astype(BF16).reshape(n_ex, per_peer, width)
    x_send[1] = dot(chosen, out_grad[...]).astype(BF16).reshape(n_ex, per_peer, width)
    y_send[...] = jnp.zeros(y_send.shape, BF16)
    stage[2 * total_pairs] = jnp.zeros((BS, LANES), BF16)
    dense[blocks // 2] = jnp.zeros((BS, LANES), F32)

    pl.semaphore_wait(barrier, n_dp - 1 + n_ex - 1)

    def x_copy(which, i):
        return pltpu.make_async_remote_copy(
            src_ref=x_send.at[which, peer(i)],
            dst_ref=x_got.at[which, my_ex],
            send_sem=x_ssem.at[which, i - 1],
            recv_sem=x_rsem.at[which, i - 1],
            device_id={"expert": peer(i)},
            device_id_type=pl.DeviceIdType.MESH,
        )

    def y_copy(which, i):
        return pltpu.make_async_remote_copy(
            src_ref=y_send.at[which, peer(i)],
            dst_ref=y_got.at[which, my_ex],
            send_sem=y_ssem.at[which, i - 1],
            recv_sem=y_rsem.at[which, i - 1],
            device_id={"expert": peer(i)},
            device_id_type=pl.DeviceIdType.MESH,
        )

    def w_copy(c, i):
        return pltpu.make_async_remote_copy(
            src_ref=own.at[c],
            dst_ref=held.at[c, i - 1],
            send_sem=w_ssem.at[c, i - 1],
            recv_sem=w_rsem.at[c, i - 1],
            device_id={"dp": ahead(i)},
            device_id_type=pl.DeviceIdType.MESH,
        )

    def g_copy(c, i):
        return pltpu.make_async_remote_copy(
            src_ref=held.at[c, i - 1],
            dst_ref=got.at[c, i - 1],
            send_sem=g_ssem.at[c, i - 1],
            recv_sem=g_rsem.at[c, i - 1],
            device_id={"dp": ahead(i)},
            device_id_type=pl.DeviceIdType.MESH,
        )

    def r_copy(i):
        return pltpu.make_async_remote_copy(
            src_ref=r_send,
            dst_ref=r_got.at[i - 1],
            send_sem=r_ssem.at[i - 1],
            recv_sem=r_rsem.at[i - 1],
            device_id={"dp": ahead(i)},
            device_id_type=pl.DeviceIdType.MESH,
        )

    loop(1, n_ex, lambda i: x_copy(0, i).start())
    for i in range(1, n_dp):
        w_copy(0, i).start()
    loop(1, n_ex, lambda i: x_copy(1, i).start())

    def send_weights(c):
        for i in range(1, n_dp):
            w_copy(c, i).start()

    loop(1, 3 * members, send_weights)
    for which in range(2):
        x_got[which, my_ex] = x_send[which, my_ex]

    low = lax.broadcasted_iota(jnp.int32, (BS, LANES), 1) < BS

    def load_stage(c):
        def put(base, tile):
            stage[base] = tile
            stage[total_pairs + base] = pltpu.roll(tile.astype(F32), BS, 1).astype(BF16)

        loop(0, pairs, lambda q: put(my_dp * pairs + q, own[c, q]))
        for i in range(1, n_dp):
            w_copy(c, i).wait_recv()
            loop(0, pairs, lambda q: put(behind(i) * pairs + q, held[c, i - 1, q]))

    def assemble(c, target, row_blocks, col_blocks):
        load_stage(c)

        def one_row(r):
            start = pl.multiple_of(r * BS, BS)
            for k in range(col_blocks // 2):
                at = c * blocks + r * col_blocks + 2 * k
                tile = jnp.where(low, stage[place_ref[at]], stage[place_ref[at + 1]])
                target[pl.ds(start, BS), k * LANES : (k + 1) * LANES] = tile

        loop(0, row_blocks, one_row)

    def dense_grad(left, right, row_blocks):
        height = row_blocks * BS
        step = 512 if height % 512 == 0 else height
        for col in range(0, right.shape[1], 2 * LANES):
            for row in range(0, height, step):
                product = dot(
                    left[:, row : row + step], right[:, col : col + 2 * LANES], ((0,), (0,))
                )
                for half in range(2):
                    base = (col // LANES + half) * row_blocks + row // BS
                    dense[base : base + step // BS] = product[
                        :, half * LANES : (half + 1) * LANES
                    ].reshape(step // BS, BS, LANES)

    def extract(c):
        def tile(d, q):
            at = c * slots + d * 2 * pairs + q
            code0 = pick_ref[at]
            code1 = pick_ref[at + pairs]
            first = dense[code0 // 2]
            second = dense[code1 // 2]
            side0 = jnp.full((BS, LANES), code0 % 2, jnp.int32)
            side1 = jnp.full((BS, LANES), code1 % 2, jnp.int32)
            first = jnp.where(side0 == 0, first, pltpu.roll(first, BS, 1))
            second = jnp.where(side1 == 1, second, pltpu.roll(second, BS, 1))
            return jnp.where(low, first, second)

        for i in range(1, n_dp):

            def fill(q):
                held[c, i - 1, q] = tile(ahead(i), q).astype(BF16)

            loop(0, pairs, fill)
            g_copy(c, i).start()

        def keep(q):
            grads[c, q] = tile(my_dp, q)

        loop(0, pairs, keep)

    def order(e):
        at = lax.broadcasted_iota(jnp.int32, (expert_rows, all_rows), 0)
        col = lax.broadcasted_iota(jnp.int32, (expert_rows, all_rows), 1)
        wanted = (at // cap) * per_peer + e * cap + at % cap
        return (col == wanted).astype(F32).astype(BF16)

    def order_back(e):
        col = lax.broadcasted_iota(jnp.int32, (all_rows, expert_rows), 1)
        at = lax.broadcasted_iota(jnp.int32, (all_rows, expert_rows), 0)
        wanted = (col // cap) * per_peer + e * cap + col % cap
        return (at == wanted).astype(F32).astype(BF16)

    def add_part(which, e, part):
        back = dot(order_back(e), part).reshape(n_ex, per_peer, width)
        y_send[which] = (y_send[which].astype(F32) + back).astype(BF16)

    def send_back(which):
        loop(1, n_ex, lambda i: y_copy(which, i).start())
        y_got[which, my_ex] = y_send[which, my_ex]

    def one_expert(e):
        c = 3 * e
        assemble(c, w_gate, in_blocks, hid_blocks)

        @pl.when(e == 0)
        def _():
            loop(1, n_ex, lambda i: x_copy(0, i).wait_recv())

        rows[...] = dot(order(e), x_got[0].reshape(all_rows, width)).astype(BF16)
        pre_gate[...] = dot(rows[...], w_gate[...])
        gating = sigma(
            jnp.sum(rows[...].astype(F32) * router[e], axis=1, keepdims=True)
        )
        assemble(c + 1, w_up, in_blocks, hid_blocks)
        pre_up[...] = dot(rows[...], w_up[...])
        gate = pre_gate[...]
        hidden[...] = (gate * sigma(gate) * pre_up[...]).astype(BF16)

        @pl.when(e == 0)
        def _():
            loop(1, n_ex, lambda i: x_copy(1, i).wait_recv())

        grad_rows = dot(order(e), x_got[1].reshape(all_rows, width))
        scaled[...] = (gating * grad_rows).astype(BF16)
        dense_grad(hidden, scaled, hid_blocks)
        assemble(c + 2, w_down, hid_blocks, in_blocks)
        extract(c + 2)
        outs[...] = dot(hidden[...], w_down[...])
        add_part(0, e, (gating * outs[...]).astype(BF16))
        grad_rows = dot(order(e), x_got[1].reshape(all_rows, width))
        logit = (
            jnp.sum(grad_rows * outs[...], axis=1, keepdims=True) * gating * (1.0 - gating)
        )
        r_send[e] = jnp.sum(rows[...].astype(F32) * logit, axis=0, keepdims=True)

        @pl.when(e == members - 1)
        def _():
            for i in range(1, n_dp):
                r_copy(i).start()
            send_back(0)

        hidden_grad = dot(scaled[...], w_down[...], ((1,), (1,)))
        gate = pre_gate[...]
        sig = sigma(gate)
        gate_grad = hidden_grad * pre_up[...] * sig * (1.0 + gate * (1.0 - sig))
        up_grad = hidden_grad * gate * sig
        pre_gate[...] = gate_grad
        pre_up[...] = up_grad
        dense_grad(rows, pre_gate[...].astype(BF16), in_blocks)
        extract(c)
        dense_grad(rows, pre_up[...].astype(BF16), in_blocks)
        extract(c + 1)
        part = dot(pre_gate[...].astype(BF16), w_gate[...], ((1,), (1,)))
        part = part + dot(pre_up[...].astype(BF16), w_up[...], ((1,), (1,)))
        add_part(1, e, (part + logit * router[e]).astype(BF16))

    loop(0, members, one_expert)
    send_back(1)

    placed = (
        lax.broadcasted_iota(jnp.int32, (tokens.shape[0], all_rows), 0) == picks_row[...]
    ).astype(F32).astype(BF16)
    loop(1, n_ex, lambda i: y_copy(0, i).wait_recv())
    layer_out[...] = dot(placed, y_got[0].reshape(all_rows, width)).astype(BF16)
    loop(1, n_ex, lambda i: y_copy(1, i).wait_recv())
    input_grad[...] = dot(placed, y_got[1].reshape(all_rows, width)).astype(BF16)

    for i in range(1, n_dp):
        r_copy(i).wait()
    share = width // n_dp
    mine = pl.ds(pl.multiple_of(my_dp * share, share), share)
    for e in range(members):
        router_total = r_send[e, :, mine]
        for i in range(1, n_dp):
            router_total = router_total + r_got[i - 1, e, :, mine]
        router_out[e] = router_total

    def finish(c):
        for i in range(1, n_dp):
            g_copy(c, i).wait_recv()

        def add(q):
            total = grads[c, q]
            for i in range(1, n_dp):
                total = total + got[c, i - 1, q].astype(F32)
            grads[c, q] = total

        loop(0, pairs, add)

    def finish_expert(e):
        for m in (2, 0, 1):
            finish(3 * e + m)

    loop(0, members, finish_expert)

    def drain_weights(c):
        for i in range(1, n_dp):
            w_copy(c, i).wait_send()
            g_copy(c, i).wait_send()

    loop(0, 3 * members, drain_weights)

    def drain_rows(i):
        for which in range(2):
            x_copy(which, i).wait_send()
            y_copy(which, i).wait_send()

    loop(1, n_ex, drain_rows)


def body(tokens, out_grad, token_picks, router, kept_blocks, masters, scores):
    members = kept_blocks.shape[0]
    slots = kept_blocks.shape[2]
    n_ex = lax.axis_size("expert")
    n_dp = lax.axis_size("dp")
    cap = token_picks.shape[2]
    width = tokens.shape[1]
    in_blocks = width // BS
    hid_blocks = FF // BS
    blocks = in_blocks * hid_blocks
    local = masters.shape[2]
    pairs = local // 2
    total_pairs = pairs * n_dp
    chunks = 3 * members
    all_rows = n_ex * members * cap
    expert_rows = n_ex * cap

    kept = kept_blocks.reshape(chunks, slots)
    numbers = jnp.arange(blocks, dtype=jnp.int32)
    hits = kept[:, None, :] == numbers[None, :, None]
    slot_of = jnp.sum(
        jnp.where(hits, jnp.arange(slots, dtype=jnp.int32) + 1, 0), axis=2
    ) - 1
    within = slot_of % local
    flipped = (within // pairs) != (numbers % 2)[None, :]
    place = (slot_of // local) * pairs + within % pairs + jnp.where(flipped, total_pairs, 0)
    place = jnp.where(slot_of >= 0, place, 2 * total_pairs).reshape(-1)

    col_counts = jnp.array([hid_blocks, hid_blocks, in_blocks] * members, jnp.int32)[:, None]
    row_counts = jnp.array([in_blocks, in_blocks, hid_blocks] * members, jnp.int32)[:, None]
    block_row = kept // col_counts
    block_col = kept % col_counts
    code = ((block_col // 2) * row_counts + block_row) * 2 + block_col % 2
    code = jnp.where(kept < blocks, code, blocks).reshape(-1)

    own = masters.astype(BF16).reshape(chunks, 2, pairs, BS, BS)
    own = own.transpose(0, 2, 3, 1, 4).reshape(chunks, pairs, BS, LANES)
    picks = token_picks[0].reshape(-1)
    router_rows = router.T.astype(F32).reshape(members, 1, width)

    vmem = pl.BlockSpec(memory_space=pltpu.VMEM)
    smem = pl.BlockSpec(memory_space=pltpu.SMEM)
    dma = pltpu.SemaphoreType.DMA
    layer_out, input_grad, grads, router_grad = pl.pallas_call(
        functools.partial(kernel, (n_dp, n_ex, members, cap)),
        out_shape=(
            jax.ShapeDtypeStruct(tokens.shape, BF16),
            jax.ShapeDtypeStruct(tokens.shape, BF16),
            jax.ShapeDtypeStruct((chunks, pairs, BS, LANES), F32),
            jax.ShapeDtypeStruct((members, 1, width // n_dp), F32),
        ),
        in_specs=[smem, smem] + [vmem] * 6,
        out_specs=[vmem] * 4,
        scratch_shapes=[
            pltpu.VMEM((chunks, n_dp - 1, pairs, BS, LANES), BF16),
            pltpu.VMEM((2 * total_pairs + 1, BS, LANES), BF16),
            pltpu.VMEM((width, FF), BF16),
            pltpu.VMEM((width, FF), BF16),
            pltpu.VMEM((FF, width), BF16),
            pltpu.VMEM((blocks // 2 + 1, BS, LANES), F32),
            pltpu.VMEM((chunks, n_dp - 1, pairs, BS, LANES), BF16),
            pltpu.VMEM((2, n_ex, members * cap, width), BF16),
            pltpu.VMEM((2, n_ex, members * cap, width), BF16),
            pltpu.VMEM((2, n_ex, members * cap, width), BF16),
            pltpu.VMEM((2, n_ex, members * cap, width), BF16),
            pltpu.VMEM((expert_rows, width), BF16),
            pltpu.VMEM((expert_rows, width), BF16),
            pltpu.VMEM((expert_rows, FF), BF16),
            pltpu.VMEM((expert_rows, FF), F32),
            pltpu.VMEM((expert_rows, FF), F32),
            pltpu.VMEM((expert_rows, width), F32),
            pltpu.VMEM((members, 1, width), F32),
            pltpu.VMEM((n_dp - 1, members, 1, width), F32),
            dma((chunks, n_dp - 1)),
            dma((chunks, n_dp - 1)),
            dma((chunks, n_dp - 1)),
            dma((chunks, n_dp - 1)),
            dma((2, n_ex - 1)),
            dma((2, n_ex - 1)),
            dma((2, n_ex - 1)),
            dma((2, n_ex - 1)),
            dma((n_dp - 1,)),
            dma((n_dp - 1,)),
        ],
        compiler_params=pltpu.CompilerParams(
            collective_id=0, has_side_effects=True, vmem_limit_bytes=62 * 1024 * 1024
        ),
    )(
        place,
        code,
        picks.reshape(all_rows, 1),
        picks.reshape(1, all_rows),
        tokens,
        out_grad,
        router_rows,
        own,
    )

    summed = grads.reshape(members, 3, pairs, BS, 2, BS).transpose(0, 1, 4, 2, 3, 5)
    summed = summed.reshape(members, 3, local, BS * BS)
    master_new = masters - LEARN_RATE * summed
    score_new = scores - SCORE_RATE * jnp.sum(masters * summed, axis=-1)
    return layer_out, input_grad, master_new, score_new, router_grad.reshape(members, -1).T


def solution(mesh):
    return jax.shard_map(
        body,
        mesh=mesh,
        in_specs=(
            P(("dp", "expert"), None),
            P(("dp", "expert"), None),
            P(("dp", "expert"), None, None),
            P(None, "expert"),
            P("expert", None, None),
            P("expert", None, "dp", None),
            P("expert", None, "dp"),
        ),
        out_specs=(
            P(("dp", "expert"), None),
            P(("dp", "expert"), None),
            P("expert", None, "dp", None),
            P("expert", None, "dp"),
            P("dp", "expert"),
        ),
        check_vma=False,
    )
```

time: 863 us -> 206 us (0.24)
  local copies, waits for them, and re-layouts: 385 us -> 44.1 us
  waiting for transfers between devices: 258 us -> 0 us
  Pallas kernels: 0 us -> 150 us
  other arithmetic: 102 us -> 10.9 us
  matrix products: 75.2 us -> 0 us
  starting transfers between devices: 19.2 us -> 0 us
  between operations: 15.6 us -> 0.71 us
    unnamed x5 -> x0, waiting for transfers between devices: 197 us -> none
    pallas_call x0 -> x1, Pallas kernels: none -> 150 us  [body(): pl.pallas_call(functools.partial(kernel, (n_dp, n_ex, members, cap)), out...]
    gather x14 -> x0, local copies, waits for them, and re-layouts: 119 us -> none  [the longest x6 71.8 us: block_matrix(): jnp.take(padded, slot_of, axis=0)]
    dot_general x22 -> x0, matrix products: 75.2 us -> none  [the longest x6 43 us: weight_grad(): lax.dot_general(operand, cotangent, (((0,), (0,)), ((), ())), preferred_e...]
    select_n x24 -> x3, other arithmetic: 66.2 us -> 2.1 us  [the longest x1 1.47 us: body(): code = jnp.where(kept < blocks, code, blocks).reshape(-1)]
    transpose x7 -> x1, local copies, waits for them, and re-layouts: 52.9 us -> 6.34 us  [body(): grads.reshape(members, 3, pairs, BS, 2, BS).transpose(0, 1, 4, 2, 3, 5)]
    all_gather x1 -> x0, waiting for transfers between devices: 40.7 us -> none  [body(): lax.all_gather(masters.astype(jnp.bfloat16), 'dp', axis=2, tiled=True)]
    unnamed x150 -> x14, local copies, waits for them, and re-layouts: 43.3 us -> 5.25 us
  transfers between devices with their start and end apart: 7 -> 0, of which waited for: 5 -> 0; matrix products, arithmetic and copies ran while one was open for 27% -> 0% of each run, Pallas kernels for 0% -> 0%
where the time goes in v1:
time: 206 us; the launch traced here: 205 us
  Pallas kernels  150 us (73%)
  local copies, waits for them, and re-layouts  44.1 us (21%)
  other arithmetic  10.9 us (5%)
    pallas_call x1, Pallas kernels, body(): pl.pallas_call(functools.partial(kernel, (n_dp, n_ex, members, cap)), out...  150 us
    reshape x2, local copies, waits for them, and re-layouts, body(): own = masters.astype(BF16).reshape(chunks, 2, pairs, BS, BS)  11.2 us
    reshape x1, local copies, waits for them, and re-layouts, body(): grads.reshape(members, 3, pairs, BS, 2, BS).transpose(0, 1, 4, 2, 3, 5)  7.11 us
    transpose x1, local copies, waits for them, and re-layouts, body(): grads.reshape(members, 3, pairs, BS, 2, BS).transpose(0, 1, 4, 2, 3, 5)  6.34 us
    reshape x1, local copies, waits for them, and re-layouts, body(): own = own.transpose(0, 2, 3, 1, 4).reshape(chunks, pairs, BS, LANES)  6.28 us
    reshape x1, local copies, waits for them, and re-layouts, body(): summed = summed.reshape(members, 3, local, BS * BS)  5.98 us
    unnamed x14, local copies, waits for them, and re-layouts  5.25 us
    reduce_sum x1, other arithmetic, body(): score_new = scores - SCORE_RATE * jnp.sum(masters * summed, axis=-1)  4.45 us

profile of v1, /device:TPU:0, one launch (start us, length us, event | category | flops | bytes accessed | tf_op | source)
XLA Modules:
  0.0 205.2 jit_solution(9542723269580209994)
XLA Ops:
  0.7 0.7 copy.35
  1.4 1.5 fusion.14.pick_ref
  2.8 0.4 select_reduce_fusion
  3.2 0.8 copy.37
  4.0 0.6 reshape_reshape_squeeze.7.picks_row
  4.6 0.6 fusion.3.place_ref
  5.2 0.7 convert_bitcast_fusion
  5.9 0.6 reshape.75.router
  6.5 0.7 reshape_reshape_squeeze.8.picks_col
  7.3 3.2 %convert_element_type.8 = bf16[2,3,32,4096]{3,2,1,0:T(8,128)(2,1)} convert(f32[2,3,32,4096]{3,2,1,0:T(8,128)} %param.14) | non-fusion elementwise | flops 786432 | bytes 4718592 | tf_op jit(solution)/shard_map/convert_element_type | solution.py:422
  10.5 4.3 %reshape.69 = bf16[6,2,16,64,64]{4,3,2,1,0:T(8,128)(2,1)S(1)} reshape(bf16[2,3,32,4096]{3,2,1,0:T(8,128)(2,1)} %convert_element_type.8) | data formatting | bytes 3145728 | tf_op jit(solution)/shard_map/reshape | solution.py:422
  14.8 6.8 %copy.48 = bf16[6,2,16,64,64]{4,1,3,2,0:T(2,128)(2,1)} copy(bf16[6,2,16,64,64]{4,3,2,1,0:T(8,128)(2,1)S(1)} %reshape.69) | data formatting | bytes 3145728 | tf_op jit(solution)/shard_map/reshape | solution.py:422
  21.7 6.3 %reshape.70.own = bf16[6,16,64,128]{3,2,1,0:T(8,128)(2,1)} reshape(bf16[6,16,64,2,64]{4,3,2,1,0:T(2,128)(2,1)} %bitcast.36) | data formatting | bytes 3145728 | tf_op jit(solution)/shard_map/reshape | solution.py:423
  27.9 149.6 %shard_map.128 = (bf16[256,2048]{1,0:T(8,128)(2,1)}, bf16[256,2048]{1,0:T(8,128)(2,1)}, f32[6,16,64,128]{3,2,1,0:T(8,128)}, f32[2,1,512]{2,1,0:T(1,128)}) custom-call(s32[2304]{0:T(1024)} %fusion.3.place_ref, s32[768]{0:T(1024)} %fusion.14.pick_ref, s32[128,1]{1,0:T(8,128)} %reshape_reshape_squeeze.8.picks_col, s32[1,128]{1,0:T(1,128)} %reshape_reshape_squeeze.7.picks_row, ...), custom_call_target="tpu_custom_call" | custom-call | tf_op jit(solution)/shard_map/pallas_call | solution.py:430
  177.5 1.3 copy.49
  178.8 7.1 %reshape.71 = f32[2,3,16,64,2,64]{5,4,3,2,1,0:T(2,128)} reshape(f32[6,16,64,128]{3,2,1,0:T(8,128)} %get-tuple-element.11) | data formatting | bytes 6291456 | tf_op jit(solution)/shard_map/reshape | solution.py:485
  185.9 6.3 %copy.41 = f32[2,3,2,16,64,64]{5,4,3,2,1,0:T(8,128)} copy(f32[2,3,2,16,64,64]{5,2,4,3,1,0:T(2,128)} %bitcast.35) | data formatting | bytes 6291456 | tf_op jit(solution)/shard_map/transpose | solution.py:485
  192.3 0.0 copy-start
  192.3 6.0 %reshape.72 = f32[2,3,32,4096]{3,2,1,0:T(8,128)} reshape(f32[2,3,2,16,64,64]{5,4,3,2,1,0:T(8,128)} %copy.41) | data formatting | bytes 6291456 | tf_op jit(solution)/shard_map/reshape | solution.py:486
  198.2 0.0 copy-done
  198.2 0.0 copy-start.3
  198.2 0.0 copy-start.2
  198.2 0.0 copy-start.1
  198.3 4.4 %multiply_reduce_fusion = (f32[2,3,32]{2,1,0:T(4,128)S(1)}, f32[2,3,32,4096]{3,2,1,0:T(8,128)}) fusion(f32[2,3,32,4096]{3,2,1,0:T(8,128)S(1)} %copy-done, f32[2,3,32,4096]{3,2,1,0:T(8,128)} %reshape.72), kind=kLoop, calls=%fused_computation.1 | loop fusion | flops 3145536 | bytes 9437952 | tf_op jit(solution)/shard_map/reduce_sum | solution.py:488
  202.7 0.0 copy-done.3
  202.7 0.6 copy.43
  203.3 0.0 copy-done.2
  203.3 1.0 copy.52
  204.3 0.0 copy-done.1
  204.3 1.0 copy.53
  (9 shorter events, 0.0 us)
Async XLA Ops:
  192.3 6.0 %copy-start = (f32[2,3,32,4096]{3,2,1,0:T(8,128)S(1)}, f32[2,3,32,4096]{3,2,1,0:T(8,128)}, u32[]{:S(2)}) copy-start(f32[2,3,32,4096]{3,2,1,0:T(8,128)} %param.14) | copy-start | bytes 9437188
  198.2 4.5 %copy-start.3 = (f32[2,3,32]{2,0,1:T(2,128)S(1)}, f32[2,3,32]{2,0,1:T(2,128)}, u32[]{:S(2)}) copy-start(f32[2,3,32]{2,0,1:T(2,128)} %param.15) | copy-start | bytes 2308
  198.2 5.1 %copy-start.2 = (bf16[256,2048]{1,0:T(8,128)(2,1)S(1)}, bf16[256,2048]{1,0:T(8,128)(2,1)}, u32[]{:S(2)}) copy-start(bf16[256,2048]{1,0:T(8,128)(2,1)} %get-tuple-element.30) | copy-start | bytes 3145732
  198.2 6.0 %copy-start.1 = (bf16[256,2048]{1,0:T(8,128)(2,1)S(1)}, bf16[256,2048]{1,0:T(8,128)(2,1)}, u32[]{:S(2)}) copy-start(bf16[256,2048]{1,0:T(8,128)(2,1)} %get-tuple-element.31) | copy-start | bytes 3145732
